TPU v7x, 32 devices: a whole 2x2x4 slice. The times are simulated.
32 devices in a mesh: row: 4 (over y, core), col: 8 (over z, x).
Axes of the slice: x: 2, y: 2, z: 4, core: 2. Of those that a mesh axis runs over, the one named last changes fastest.
Arguments:
- points: float32 [4, 4, 256, 128], P(None, 'row'), may hold values from -1 to 1
- rhs: float32 [4, 4, 256, 256], P(None, 'row', None, 'col'), may hold values from -6 to 6
Outputs:
- factored: float32 [4, 4, 256, 2, 8, 256], P(None, 'row', None, None, 'col')
- solved: float32 [4, 4, 256, 256], P(None, 'row', None, 'col')
All inputs are finite; a program needn't handle non-finite values.
Results may differ from a plain program's by a relative error of at most 0.0003.
Values sent between devices are 32-bit elements; how exact they have to be, the bound alone decides.
A program may use at most 64 MiB of HBM per device.

v0:
```python
import jax
import jax.numpy as jnp
from jax import lax
from jax.sharding import PartitionSpec as P

PANELS = 2
SCALE = 3.0
NUGGET = 1.0
HIGHEST = lax.Precision.HIGHEST


def from_root(block, axis, owner):
    block = jnp.where(lax.axis_index(axis) == owner, block, jnp.zeros_like(block))
    return lax.psum(block, axis)


def kernel_tiles(left_points, right_points, left_index, right_index):
    feature_dim = left_points.shape[-1]
    left_sq = jnp.sum(left_points * left_points, axis=-1)
    right_sq = jnp.sum(right_points * right_points, axis=-1)
    inner_prod = jnp.einsum("ipf,jqf->ipjq", left_points, right_points, precision=HIGHEST)
    distance = left_sq[:, :, None, None] + right_sq[None, None, :, :] - 2.0 * inner_prod
    diagonal_hit = (left_index[:, :, None, None] == right_index[None, None, :, :]).astype(
        jnp.float32
    )
    return jnp.exp(-SCALE / feature_dim * distance) + NUGGET * diagonal_hit


def advance(current, panel_tiles, inverse, pivot_rhs, tile_of_row, which_panel):
    answer = jnp.dot(inverse, pivot_rhs, precision=HIGHEST)
    change = jnp.einsum("ipq,qn->ipn", panel_tiles, answer, precision=HIGHEST)
    below_rows = (tile_of_row > which_panel)[:, None, None]
    return (jnp.where(below_rows, current - change, current), answer)


def per_device(points, rhs):
    rows_n = lax.axis_size("row")
    cols_n = lax.axis_size("col")
    row_id = lax.axis_index("row")
    col_id = lax.axis_index("col")
    tile_rows = points.shape[0]
    tile_size = points.shape[2]
    feature_dim = points.shape[3]
    tile_cols = tile_rows * rows_n // cols_n
    stride = cols_n // rows_n
    row_points = points[:, 0]
    tile_of_row = jnp.arange(tile_rows, dtype=jnp.int32) * rows_n + row_id
    tile_of_col = jnp.arange(tile_cols, dtype=jnp.int32) * cols_n + col_id
    offsets = jnp.arange(tile_size, dtype=jnp.int32)
    row_index = tile_of_row[:, None] * tile_size + offsets[None, :]
    col_index = tile_of_col[:, None] * tile_size + offsets[None, :]
    grouped = row_points.reshape(tile_cols, stride, tile_size, feature_dim)
    chosen = lax.dynamic_index_in_dim(grouped, col_id // rows_n, 1, keepdims=False)
    col_points = from_root(chosen, "row", col_id % rows_n)
    kernel_grid = kernel_tiles(row_points, col_points, row_index, col_index)
    current = rhs[:, 0]
    identity = jnp.eye(tile_size, dtype=jnp.float32)
    row_panels = []
    answers = []
    for which_panel in range(PANELS):
        slot_a = which_panel // rows_n
        root_r = which_panel % rows_n
        slot_b = which_panel // cols_n
        root_c = which_panel % cols_n
        column_slab = kernel_grid[:, :, slot_b, :]
        pivot_tile, pivot_rhs = (
            from_root(column_slab[slot_a], "row", root_r),
            from_root(current[slot_a], "row", root_r),
        )
        factor = jnp.linalg.cholesky(pivot_tile)
        inverse = jax.scipy.linalg.solve_triangular(factor, identity, lower=True)
        panel_tiles = jnp.einsum("ipq,sq->ips", column_slab, inverse, precision=HIGHEST)
        panel_tiles, inverse = (
            from_root(panel_tiles, "col", root_c),
            from_root(inverse, "col", root_c),
        )
        grouped_panel = panel_tiles.reshape(tile_cols, stride, tile_size, tile_size)
        chosen_panel = lax.dynamic_index_in_dim(grouped_panel, col_id // rows_n, 1, keepdims=False)
        panel_cols = from_root(chosen_panel, "row", col_id % rows_n)
        kernel_grid = kernel_grid - jnp.einsum(
            "ipk,jqk->ipjq", panel_tiles, panel_cols, precision=HIGHEST
        )
        current, answer = advance(
            current, panel_tiles, inverse, pivot_rhs, tile_of_row, which_panel
        )
        row_panels.append(panel_tiles)
        answers.append(answer)
    solved = current
    for which_panel in range(PANELS):
        solved = jnp.where(
            (tile_of_row == which_panel)[:, None, None], answers[which_panel][None], solved
        )
    trailing_mask = (tile_of_row >= PANELS)[:, None, None, None] & (tile_of_col >= PANELS)[
        None, None, :, None
    ]
    factored = jnp.where(trailing_mask, kernel_grid, 0.0)
    beneath = row_index[:, :, None, None] >= col_index[None, None, :, :]
    for which_panel in range(PANELS):
        pick = beneath & (tile_of_col == which_panel)[None, None, :, None]
        factored = jnp.where(pick, row_panels[which_panel][:, :, None, :], factored)
    return (factored[:, None, :, :, None, :], solved[:, None])


def solution(mesh):
    return jax.shard_map(
        per_device,
        mesh=mesh,
        in_specs=(P(None, "row", None, None), P(None, "row", None, "col")),
        out_specs=(P(None, "row", None, None, "col", None), P(None, "row", None, "col")),
        check_vma=False,
    )
```

profile of v0, /device:TPU:0, one launch (start us, length us, event | category | flops | bytes accessed | tf_op | source)
XLA Modules:
  0.0 532.5 jit_solution(501918577944356869)
XLA Ops:
  10.4 35.2 %all-reduce.10.cloned.1.call-done = f32[2,256,128]{2,1,0:T(8,128)} async-done(((f32[2,256,128]{2,1,0:T(8,128)}), f32[2,256,128]{2,1,0:T(8,128)}) %all-reduce.10.cloned.1.call-update) | async-done | bytes 262160 | tf_op jit(solution)/shard_map/psum | solution.py:14
  46.7 3.4 fusion.2
  51.4 31.7 %all-reduce.12.cloned.1.call-done = f32[256,256]{0,1:T(8,128)} async-done(((f32[256,256]{0,1:T(8,128)}), f32[256,256]{0,1:T(8,128)}) %all-reduce.12.cloned.1.call-update) | async-done | bytes 262160 | tf_op jit(solution)/shard_map/psum | solution.py:14
  85.2 11.7 %cholesky.130 = f32[128,128]{1,0:T(8,128)S(1)} custom-call(f32[128,128]{1,0:T(8,128)S(1)} %cholesky.194), custom_call_target="Cholesky" | custom-call | tf_op jit(solution)/shard_map/jit(cholesky)/cholesky | solution.py:70
  96.9 9.8 %custom-call.13 = f32[1,128,128]{1,2,0:T(8,128)S(1)} custom-call(f32[1,128,128]{2,1,0:T(8,128)S(1)} %get-tuple-element.54), custom_call_target="InvertDiagBlocksLowerTriangular" | custom-call | tf_op jit(solution)/shard_map/jit(cholesky)/cholesky | solution.py:70
  107.3 11.7 %cholesky.147 = f32[128,128]{1,0:T(8,128)S(1)} custom-call(f32[128,128]{1,0:T(8,128)S(1)} %convolution_subtract_fusion.6), custom_call_target="Cholesky" | custom-call | tf_op jit(solution)/shard_map/jit(cholesky)/cholesky | solution.py:70
  121.1 4.6 while.4
  125.7 19.7 %custom-call.14 = f32[2,128,128]{1,2,0:T(8,128)S(1)} custom-call(f32[2,128,128]{2,1,0:T(8,128)S(1)} %get-tuple-element.18), custom_call_target="InvertDiagBlocksLowerTriangular" | custom-call | tf_op jit(solution)/shard_map/jit(_solve_triangular)/triangular_solve | solution.py:71
  146.3 2.9 convolution_select_fusion.1
  149.3 78.0 %all-reduce.14.cloned.1.call-done = f32[4,256,256]{2,1,0:T(8,128)} async-done(((f32[4,256,256]{2,1,0:T(8,128)}), f32[4,256,256]{2,1,0:T(8,128)}) %all-reduce.14.cloned.1.call-update) | async-done | bytes 1048592 | tf_op jit(solution)/shard_map/psum | solution.py:14
  227.3 2.0 fusion.11
  229.4 33.1 %all-reduce.16.cloned.1.call-done = f32[2,256,256]{2,1,0:T(8,128)} async-done(((f32[2,256,256]{2,1,0:T(8,128)}), f32[2,256,256]{2,1,0:T(8,128)}) %all-reduce.16.cloned.1.call-update) | async-done | bytes 524304 | tf_op jit(solution)/shard_map/psum | solution.py:14
  262.5 3.6 convolution_subtract_fusion
  268.7 30.2 %all-reduce.18.cloned.1.call-done = f32[256,256]{0,1:T(8,128)} async-done(((f32[256,256]{0,1:T(8,128)}), f32[256,256]{0,1:T(8,128)}) %all-reduce.18.cloned.1.call-update) | async-done | bytes 262160 | tf_op jit(solution)/shard_map/psum | solution.py:14
  299.0 1.8 copy.23
  302.5 11.7 %cholesky.164 = f32[128,128]{1,0:T(8,128)S(1)} custom-call(f32[128,128]{1,0:T(8,128)S(1)} %cholesky.197), custom_call_target="Cholesky" | custom-call | tf_op jit(solution)/shard_map/jit(cholesky)/cholesky | solution.py:70
  315.0 10.4 %custom-call.15 = f32[1,128,128]{1,2,0:T(8,128)} custom-call(f32[1,128,128]{2,1,0:T(8,128)S(1)} %get-tuple-element.50), custom_call_target="InvertDiagBlocksLowerTriangular" | custom-call | tf_op jit(solution)/shard_map/jit(cholesky)/cholesky | solution.py:70
  326.1 1.7 constant_dynamic-update-slice_fusion
  328.9 11.7 %cholesky.181 = f32[128,128]{1,0:T(8,128)S(1)} custom-call(f32[128,128]{1,0:T(8,128)S(1)} %convolution_subtract_fusion.5), custom_call_target="Cholesky" | custom-call | tf_op jit(solution)/shard_map/jit(cholesky)/cholesky | solution.py:70
  344.0 5.9 %while.5 = (s32[]{:T(128)}, f32[256,256]{1,0:T(8,128)}, s32[2,2]{1,0:T(2,128)S(1)}, f32[2,128,128]{2,1,0:T(8,128)S(1)}, s32[]{:T(128)}) while((s32[]{:T(128)}, f32[256,256]{1,0:T(8,128)}, s32[2,2]{1,0:T(2,128)S(1)}, f32[2,128,128]{2,1,0:T(8,128)S(1)}, s32[]{:T(128)}) %tuple.73), condition=%wide.while_cond.clone, body=%wide.while_body.clone.sunk | while | flops 2 | bytes 131189 | solution.py:71
  344.8 2.3 bitcast_dynamic-update-slice_fusion.5
  347.7 2.2 bitcast_dynamic-update-slice_fusion.5
  350.5 20.5 %custom-call.16 = f32[2,128,128]{1,2,0:T(8,128)S(1)} custom-call(f32[2,128,128]{2,1,0:T(8,128)} %copy-done.6), custom_call_target="InvertDiagBlocksLowerTriangular" | custom-call | tf_op jit(solution)/shard_map/jit(_solve_triangular)/triangular_solve | solution.py:71
  373.5 2.8 convolution_select_fusion
  376.4 10.7 %psum.86 = f32[256,32]{0,1:T(8,128)S(1)} all-reduce(f32[256,32]{0,1:T(8,128)S(1)} %select_bitcast_fusion.3), channel_id=1, replica_groups=mesh['row'=4,'col'=8] {'row'}, use_global_device_ids=true, to_apply=%region_15.18 | all-reduce | flops 8192 | bytes 65536 | tf_op jit(solution)/shard_map/psum | solution.py:14
  388.5 77.7 %all-reduce.22.cloned.1.call-done = (f32[4,256,256]{2,1,0:T(8,128)}, f32[256,256]{1,0:T(8,128)}, f32[256,256]{1,0:T(8,128)}) async-done(((f32[4,256,256]{2,1,0:T(8,128)}, f32[256,256]{1,0:T(8,128)}, f32[256,256]{1,0:T(8,128)}), (f32[4,256,256]{2,1,0:T(8,128)}, f32[256,256]{1,0:T(8,128)}, f32[256,256]{1,0:T(8,128)})) %all-reduce.22.cloned.1.call-update) | async-done | bytes 1572880 | tf_op jit(solution)/shard_map/psum | solution.py:14
  467.6 2.3 fusion.4
  469.9 11.3 %psum.87 = f32[256,32]{0,1:T(8,128)S(1)} all-reduce(f32[256,32]{0,1:T(8,128)S(1)} %fusion.41), channel_id=1, replica_groups=mesh['row'=4,'col'=8] {'row'}, use_global_device_ids=true, to_apply=%region_16.19 | all-reduce | flops 8192 | bytes 65536 | tf_op jit(solution)/shard_map/psum | solution.py:14
  484.7 1.7 fusion.7
  486.4 27.5 %all-reduce.20.cloned.1.call-done = f32[2,256,256]{2,1,0:T(8,128)} async-done(((f32[2,256,256]{2,1,0:T(8,128)}), f32[2,256,256]{2,1,0:T(8,128)}) %all-reduce.20.cloned.1.call-update) | async-done | bytes 524304 | tf_op jit(solution)/shard_map/psum | solution.py:14
  513.9 5.5 %select_bitcast_fusion = f32[4,1,256,2,1,256]{2,5,3,0,4,1:T(8,128)} fusion(f32[4,256,2,256]{1,3,2,0:T(8,128)S(1)} %convolution_subtract_fusion, f32[4,256,256]{2,1,0:T(8,128)S(1)} %copy-done, f32[4,256,256]{1,2,0:T(8,128)} %copy.26, f32[4,256,256]{1,2,0:T(8,128)} %copy.25, s32[2,256]{1,0:T(2,128)S(1)} %iota_add_fusion.1, s32[4,256]{1,0:T(4,128)S(1)} %iota_add_fusion, ...), kind=kOutput, calls=%fused_computation.10 | convolution fusion | flops 1614282752 | bytes 7870476 | tf_op jit(solution)/shard_map/ipk,jqk->ipjq/dot_general | solution.py:80
  519.4 6.0 %copy.29 = f32[4,1,256,2,1,256]{5,4,3,2,1,0:T(1,128)} copy(f32[4,1,256,2,1,256]{2,5,3,0,4,1:T(8,128)} %select_bitcast_fusion) | data formatting | bytes 4194304
  (92 shorter events, 33.5 us)
Async XLA Ops:
  7.2 38.4 %all-reduce.10.cloned.1.call-start = ((), (), s32[]{:S(2)}) async-start(), calls=%async_computation | async-start | bytes 524288 | tf_op jit(solution)/shard_map/psum | solution.py:14
  8.9 74.2 %all-reduce.12.cloned.1.call-start = ((), (), s32[]{:S(2)}) async-start(), calls=%async_computation.1 | async-start | bytes 524288 | tf_op jit(solution)/shard_map/psum | solution.py:14
  50.2 96.1 %copy-start.2 = (f32[4,256,2,256]{1,3,2,0:T(8,128)}, f32[4,256,2,256]{1,3,2,0:T(8,128)S(1)}, u32[]{:S(2)}) copy-start(f32[4,256,2,256]{1,3,2,0:T(8,128)S(1)} %fusion.2) | copy-start | bytes 6291460
  51.0 176.3 %all-reduce.14.cloned.1.call-start = ((), (), s32[]{:S(2)}) async-start(), calls=%async_computation.2 | async-start | bytes 2097152 | tf_op jit(solution)/shard_map/psum | solution.py:14
  146.3 2.9 copy-start.3
  149.2 113.3 %all-reduce.16.cloned.1.call-start = ((), (), s32[]{:S(2)}) async-start(), calls=%async_computation.3 | async-start | bytes 1048576 | tf_op jit(solution)/shard_map/psum | solution.py:14
  227.3 35.2 %copy-start.1 = (f32[4,256,256]{2,1,0:T(8,128)S(1)}, f32[4,256,256]{2,1,0:T(8,128)}, u32[]{:S(2)}) copy-start(f32[4,256,256]{2,1,0:T(8,128)} %all-reduce.14.cloned.1.call-done) | copy-start | bytes 3145732
  229.3 69.7 %all-reduce.18.cloned.1.call-start = ((), (), s32[]{:S(2)}) async-start(), calls=%async_computation.4 | async-start | bytes 524288 | tf_op jit(solution)/shard_map/psum | solution.py:14
  266.8 199.3 %all-reduce.22.cloned.1.call-start = ((), (), s32[]{:S(2)}) async-start(), calls=%async_computation.6 | async-start | bytes 3145728 | tf_op jit(solution)/shard_map/psum | solution.py:14
  301.8 0.7 copy-start.4
  349.9 0.7 copy-start.6
  373.5 2.9 copy-start.5
  376.3 137.7 %all-reduce.20.cloned.1.call-start = ((), (), s32[]{:S(2)}) async-start(), calls=%async_computation.5 | async-start | bytes 1048576 | tf_op jit(solution)/shard_map/psum | solution.py:14
  466.2 15.0 %copy-start = (f32[4,256,256]{2,1,0:T(8,128)S(1)}, f32[4,256,256]{2,1,0:T(8,128)}, u32[]{:S(2)}) copy-start(f32[4,256,256]{2,1,0:T(8,128)} %get-tuple-element.40) | copy-start | bytes 3145732
Sparse Core Ops, SparseCore 0:
  10.9 34.6 all-reduce.9
  51.1 31.9 all-reduce.11
  149.3 77.9 all-reduce.13
  229.6 32.7 all-reduce.15
  267.0 31.9 all-reduce.17
  376.4 89.7 all-reduce.21
  482.2 31.6 all-reduce.19
where the time goes:
time: 536 us; the launch traced here: 533 us
  waiting for transfers between devices  314 us (59%)
  other arithmetic  124 us (23%)
  matrix products  30.8 us (6%)
  local copies, waits for them, and re-layouts  23.4 us (4%)
  blocking collectives  22 us (4%)
  between operations  17.3 us (3%)
    psum x7, waiting for transfers between devices, from_root(): return lax.psum(block, axis)  313 us
    another operation x13, other arithmetic, per_device(): factor = jnp.linalg.cholesky(pivot_tile)  69.9 us
    another operation x5, other arithmetic, per_device(): inverse = jax.scipy.linalg.solve_triangular(factor, identity, lower=True)  40.9 us
    psum x2, blocking collectives, from_root(): return lax.psum(block, axis)  22 us
  transfers between devices with their start and end apart: 7, of which 7 were waited for; matrix products, arithmetic and copies ran while one was open for 2% of the time, Pallas kernels for 0%

commit v1 on v0

--- a/solution.py
+++ b/solution.py
@@ -11,7 +11,7 @@
 
 def from_root(block, axis, owner):
     block = jnp.where(lax.axis_index(axis) == owner, block, jnp.zeros_like(block))
-    return lax.psum(block, axis)
+    return jnp.sum(lax.all_gather(block, axis), axis=0)
 
 
 def kernel_tiles(left_points, right_points, left_index, right_index):

time: 536 us -> 652 us (1.22)
  waiting for transfers between devices: 314 us -> 419 us
  other arithmetic: 124 us -> 145 us
  blocking collectives: 22 us -> 10.9 us
    all_gather x0 -> x9, waiting for transfers between devices: none -> 419 us  [from_root(): return jnp.sum(lax.all_gather(block, axis), axis=0)]
    psum x7 -> x0, waiting for transfers between devices: 313 us -> none  [from_root(): return lax.psum(block, axis)]
    psum x2 -> x0, blocking collectives: 22 us -> none  [from_root(): return lax.psum(block, axis)]
    reduce_sum x0 -> x11, other arithmetic: none -> 19.2 us  [from_root(): return jnp.sum(lax.all_gather(block, axis), axis=0)]
    all_gather x0 -> x2, blocking collectives: none -> 10.9 us  [from_root(): return jnp.sum(lax.all_gather(block, axis), axis=0)]
  transfers between devices with their start and end apart: 7 -> 9, of which waited for: 7 -> 9; matrix products, arithmetic and copies ran while one was open for 2% -> 3% of each run, Pallas kernels for 0% -> 0%
where the time goes in v1:
time: 652 us; the launch traced here: 648 us
  waiting for transfers between devices  419 us (64%)
  other arithmetic  145 us (22%)
  matrix products  28.7 us (4%)
  local copies, waits for them, and re-layouts  24.6 us (4%)
  between operations  17.2 us (3%)
  blocking collectives  10.9 us (2%)
    all_gather x9, waiting for transfers between devices, from_root(): return jnp.sum(lax.all_gather(block, axis), axis=0)  419 us
    another operation x13, other arithmetic, per_device(): factor = jnp.linalg.cholesky(pivot_tile)  76 us
    another operation x5, other arithmetic, per_device(): inverse = jax.scipy.linalg.solve_triangular(factor, identity, lower=True)  41.5 us
    reduce_sum x11, other arithmetic, from_root(): return jnp.sum(lax.all_gather(block, axis), axis=0)  19.2 us
  transfers between devices with their start and end apart: 9, of which 9 were waited for; matrix products, arithmetic and copies ran while one was open for 3% of the time, Pallas kernels for 0%

profile of v1, /device:TPU:0, one launch (start us, length us, event | category | flops | bytes accessed | tf_op | source)
XLA Modules:
  0.0 647.6 jit_solution(3749464608499495141)
XLA Ops:
  10.5 19.1 %all-gather.20.cloned.1.call-done = f32[8,1,256,128]{3,2,1,0:T(8,128)} async-done(((f32[2,1,256,128]{3,2,1,0:T(8,128)}), f32[8,1,256,128]{3,2,1,0:T(8,128)}) %all-gather.20.cloned.1.call-update) | async-done | bytes 1048592 | tf_op jit(solution)/shard_map/all_gather | solution.py:14
  31.1 2.3 fusion.2
  34.9 16.5 %all-gather.22.cloned.1.call-done = f32[4,256,1,256]{3,1,2,0:T(8,128)} async-done(((f32[1,256,1,256]{3,1,2,0:T(8,128)}), f32[4,256,1,256]{3,1,2,0:T(8,128)}) %all-gather.22.cloned.1.call-update) | async-done | bytes 1048592 | tf_op jit(solution)/shard_map/all_gather | solution.py:14
  52.9 11.7 %cholesky.130 = f32[128,128]{1,0:T(8,128)S(1)} custom-call(f32[128,128]{1,0:T(8,128)S(1)} %cholesky.194), custom_call_target="Cholesky" | custom-call | tf_op jit(solution)/shard_map/jit(cholesky)/cholesky | solution.py:70
  64.7 9.8 %custom-call.13 = f32[1,128,128]{1,2,0:T(8,128)S(1)} custom-call(f32[1,128,128]{2,1,0:T(8,128)S(1)} %get-tuple-element.53), custom_call_target="InvertDiagBlocksLowerTriangular" | custom-call | tf_op jit(solution)/shard_map/jit(cholesky)/cholesky | solution.py:70
  75.0 11.7 %cholesky.147 = f32[128,128]{1,0:T(8,128)S(1)} custom-call(f32[128,128]{1,0:T(8,128)S(1)} %convolution_subtract_fusion.6), custom_call_target="Cholesky" | custom-call | tf_op jit(solution)/shard_map/jit(cholesky)/cholesky | solution.py:70
  88.9 4.7 while.4
  93.6 19.7 %custom-call.14 = f32[2,128,128]{1,2,0:T(8,128)S(1)} custom-call(f32[2,128,128]{2,1,0:T(8,128)S(1)} %get-tuple-element.18), custom_call_target="InvertDiagBlocksLowerTriangular" | custom-call | tf_op jit(solution)/shard_map/jit(_solve_triangular)/triangular_solve | solution.py:71
  114.2 2.9 convolution_select_fusion.1
  117.2 125.0 %all-gather.24.cloned.1.call-done = f32[32,256,256]{2,1,0:T(8,128)} async-done(((f32[4,256,256]{2,1,0:T(8,128)}), f32[32,256,256]{2,1,0:T(8,128)}) %all-gather.24.cloned.1.call-update) | async-done | bytes 8388624 | tf_op jit(solution)/shard_map/all_gather | solution.py:14
  242.2 4.1 reduce_sum.121
  247.2 20.9 %all-gather.26.cloned.1.call-done = f32[8,1,256,256]{3,2,1,0:T(8,128)} async-done(((f32[2,1,256,256]{3,2,1,0:T(8,128)}), f32[8,1,256,256]{3,2,1,0:T(8,128)}) %all-gather.26.cloned.1.call-update) | async-done | bytes 2097168 | tf_op jit(solution)/shard_map/all_gather | solution.py:14
  269.9 3.5 convolution_subtract_fusion
  274.7 16.7 %all-gather.28.cloned.1.call-done = f32[4,256,1,256]{3,1,2,0:T(8,128)} async-done(((f32[1,256,1,256]{3,1,2,0:T(8,128)}), f32[4,256,1,256]{3,1,2,0:T(8,128)}) %all-gather.28.cloned.1.call-update) | async-done | bytes 1048592 | tf_op jit(solution)/shard_map/all_gather | solution.py:14
  295.8 13.2 %cholesky.164 = f32[128,128]{1,0:T(8,128)} custom-call(f32[128,128]{1,0:T(8,128)} %cholesky.197), custom_call_target="Cholesky" | custom-call | tf_op jit(solution)/shard_map/jit(cholesky)/cholesky | solution.py:70
  312.0 11.3 %custom-call.15 = f32[1,128,128]{1,2,0:T(8,128)} custom-call(f32[1,128,128]{2,1,0:T(8,128)} %get-tuple-element.49), custom_call_target="InvertDiagBlocksLowerTriangular" | custom-call | tf_op jit(solution)/shard_map/jit(cholesky)/cholesky | solution.py:70
  326.7 13.2 %cholesky.181 = f32[128,128]{1,0:T(8,128)} custom-call(f32[128,128]{1,0:T(8,128)} %convolution_subtract_fusion.5), custom_call_target="Cholesky" | custom-call | tf_op jit(solution)/shard_map/jit(cholesky)/cholesky | solution.py:70
  345.5 7.2 %while.5 = (s32[]{:T(128)}, f32[256,256]{1,0:T(8,128)}, s32[2,2]{1,0:T(2,128)S(1)}, f32[2,128,128]{2,1,0:T(8,128)}, s32[]{:T(128)}) while((s32[]{:T(128)}, f32[256,256]{1,0:T(8,128)}, s32[2,2]{1,0:T(2,128)S(1)}, f32[2,128,128]{2,1,0:T(8,128)}, s32[]{:T(128)}) %tuple.76), condition=%wide.while_cond.clone, body=%wide.while_body.clone.sunk | while | flops 2 | bytes 132705 | solution.py:71
  346.3 2.9 bitcast_dynamic-update-slice_fusion.5
  349.9 2.8 bitcast_dynamic-update-slice_fusion.5
  352.7 21.1 %custom-call.16 = f32[2,128,128]{1,2,0:T(8,128)} custom-call(f32[2,128,128]{2,1,0:T(8,128)} %get-tuple-element.19), custom_call_target="InvertDiagBlocksLowerTriangular" | custom-call | tf_op jit(solution)/shard_map/jit(_solve_triangular)/triangular_solve | solution.py:71
  377.3 2.9 convolution_select_fusion
  382.8 122.5 %all-gather.30.cloned.1.call-done = f32[32,256,256]{2,1,0:T(8,128)} async-done(((f32[4,256,256]{2,1,0:T(8,128)}), f32[32,256,256]{2,1,0:T(8,128)}) %all-gather.30.cloned.1.call-update) | async-done | bytes 8388624 | tf_op jit(solution)/shard_map/all_gather | solution.py:14
  505.3 4.1 reduce_sum.124
  510.3 5.4 all-gather.9
  515.9 39.1 %all-gather.36.cloned.1.call-done = f32[2048,256]{1,0:T(8,128)} async-done(((f32[256,256]{1,0:T(8,128)}), f32[2048,256]{1,0:T(8,128)}) %all-gather.36.cloned.1.call-update) | async-done | bytes 2097168 | tf_op jit(solution)/shard_map/all_gather | solution.py:14
  558.5 5.4 all_gather.66
  563.9 41.0 %all-gather.34.cloned.1.call-done = f32[2048,256]{1,0:T(8,128)} async-done(((f32[256,256]{1,0:T(8,128)}), f32[2048,256]{1,0:T(8,128)}) %all-gather.34.cloned.1.call-update) | async-done | bytes 2097168 | tf_op jit(solution)/shard_map/all_gather | solution.py:14
  609.0 18.5 %all-gather.32.cloned.1.call-done = f32[8,1,256,256]{3,2,1,0:T(8,128)} async-done(((f32[2,1,256,256]{3,2,1,0:T(8,128)}), f32[8,1,256,256]{3,2,1,0:T(8,128)}) %all-gather.32.cloned.1.call-update) | async-done | bytes 2097168 | tf_op jit(solution)/shard_map/all_gather | solution.py:14
  627.5 1.8 bitcast_reduce_fusion
  629.3 5.4 select_bitcast_fusion
  634.8 6.1 copy.36
  (118 shorter events, 49.2 us)
Async XLA Ops:
  7.2 23.9 %copy-start.7 = (f32[4,1,256,128]{3,2,1,0:T(8,128)S(1)}, f32[4,1,256,128]{3,2,1,0:T(8,128)}, u32[]{:S(2)}) copy-start(f32[4,1,256,128]{3,2,1,0:T(8,128)} %param.5) | copy-start | bytes 1572868
  7.2 22.4 %all-gather.20.cloned.1.call-start = ((), (), s32[]{:S(2)}) async-start(), calls=%async_computation | async-start | bytes 1310720 | tf_op jit(solution)/shard_map/all_gather | solution.py:14
  9.0 42.4 %all-gather.22.cloned.1.call-start = ((), (), s32[]{:S(2)}) async-start(), calls=%async_computation.1 | async-start | bytes 1310720 | tf_op jit(solution)/shard_map/all_gather | solution.py:14
  33.4 80.8 %copy-start.1 = (f32[4,256,2,256]{1,3,0,2:T(8,128)}, f32[4,256,2,256]{1,3,0,2:T(8,128)S(1)}, u32[]{:S(2)}) copy-start(f32[4,256,2,256]{1,3,0,2:T(8,128)S(1)} %fusion.2) | copy-start | bytes 6291460
  34.5 207.7 %all-gather.24.cloned.1.call-start = ((), (), s32[]{:S(2)}) async-start(), calls=%async_computation.2 | async-start | bytes 9437184 | tf_op jit(solution)/shard_map/all_gather | solution.py:14
  34.9 78.7 %copy-start.2 = (f32[256,256]{1,0:T(8,128)}, f32[256,256]{1,0:T(8,128)S(1)}, u32[]{:S(2)}) copy-start(f32[256,256]{1,0:T(8,128)S(1)} %fusion.19) | copy-start | bytes 786436
  114.2 132.1 %copy-start.5 = (f32[128,256]{1,0:T(8,128)}, f32[128,256]{1,0:T(8,128)S(1)}, u32[]{:S(2)}) copy-start(f32[128,256]{1,0:T(8,128)S(1)} %fusion.31) | copy-start | bytes 393220
  117.1 151.0 %all-gather.26.cloned.1.call-start = ((), (), s32[]{:S(2)}) async-start(), calls=%async_computation.3 | async-start | bytes 2621440 | tf_op jit(solution)/shard_map/all_gather | solution.py:14
  247.1 44.2 %all-gather.28.cloned.1.call-start = ((), (), s32[]{:S(2)}) async-start(), calls=%async_computation.4 | async-start | bytes 1310720 | tf_op jit(solution)/shard_map/all_gather | solution.py:14
  273.4 109.3 %copy-start = (f32[4,256,2,256]{1,3,0,2:T(8,128)}, f32[4,256,2,256]{1,3,0,2:T(8,128)S(1)}, u32[]{:S(2)}) copy-start(f32[4,256,2,256]{1,3,0,2:T(8,128)S(1)} %convolution_subtract_fusion) | copy-start | bytes 6291460
  274.4 230.8 %all-gather.30.cloned.1.call-start = ((), (), s32[]{:S(2)}) async-start(), calls=%async_computation.5 | async-start | bytes 9437184 | tf_op jit(solution)/shard_map/all_gather | solution.py:14
  294.5 0.7 copy-start.8
  295.2 78.6 %copy-start.3 = (f32[256,256]{1,0:T(8,128)S(1)}, f32[256,256]{1,0:T(8,128)}, u32[]{:S(2)}) copy-start(f32[256,256]{1,0:T(8,128)} %copy-done.2) | copy-start | bytes 786436
  374.9 2.4 copy-start.4
  376.1 4.2 copy-start.6
  380.2 174.7 %all-gather.36.cloned.1.call-start = ((), (), s32[]{:S(2)}) async-start(), calls=%async_computation.8 | async-start | bytes 2359296 | tf_op jit(solution)/shard_map/all_gather | solution.py:14
  381.0 223.9 %all-gather.34.cloned.1.call-start = ((), (), s32[]{:S(2)}) async-start(), calls=%async_computation.7 | async-start | bytes 2359296 | tf_op jit(solution)/shard_map/all_gather | solution.py:14
  382.7 244.8 %all-gather.32.cloned.1.call-start = ((), (), s32[]{:S(2)}) async-start(), calls=%async_computation.6 | async-start | bytes 2621440 | tf_op jit(solution)/shard_map/all_gather | solution.py:14
  505.3 4.9 copy-start.9
Sparse Core Ops, SparseCore 0:
  10.1 19.4 all-gather.19
  34.6 16.7 all-gather.21
  117.2 124.9 all-gather.23
  247.3 20.7 all-gather.25
  274.6 16.7 all-gather.27
  380.3 124.9 all-gather.29
  507.4 47.4 all-gather.35
  557.0 47.7 all-gather.33
  606.4 21.0 all-gather.31
